TPU v7x, 32 devices: a whole 2x2x4 slice. The times are simulated.
32 devices in a mesh: ha: 4 (over y, x), wa: 8 (over z, core).
Axes of the slice: x: 2, y: 2, z: 4, core: 2. Of those that a mesh axis runs over, the one named last changes fastest.
Arguments:
- field: bfloat16 [192, 512, 256], P('ha', 'wa'), may hold values from -41 to 41
- expand_w: bfloat16 [256, 1024], replicated, may hold values from -0.375 to 0.375
- dw_kernel: float32 [9, 1024], replicated, may hold values from -2 to 2
- project_w: bfloat16 [1024, 256], replicated, may hold values from -0.1875 to 0.1875
- blk_qkv: bfloat16 [256, 768], replicated, may hold values from -0.375 to 0.375
- blk_out: bfloat16 [256, 256], replicated, may hold values from -0.375 to 0.375
- blk_table: float32 [225, 8], replicated, may hold values from -4 to 290
- blk_index: int32 [64, 64], replicated, may hold values from 0 to 224, as said below
- blk_up: bfloat16 [256, 1024], replicated, may hold values from -0.375 to 0.375
- blk_down: bfloat16 [1024, 256], replicated, may hold values from -0.1875 to 0.1875
- grid_qkv: bfloat16 [256, 768], replicated, may hold values from -0.375 to 0.375
- grid_out: bfloat16 [256, 256], replicated, may hold values from -0.375 to 0.375
- grid_table: float32 [225, 8], replicated, may hold values from -4 to 290
- grid_index: int32 [64, 64], replicated, may hold values from 0 to 224, as said below
- grid_up: bfloat16 [256, 1024], replicated, may hold values from -0.375 to 0.375
- grid_down: bfloat16 [1024, 256], replicated, may hold values from -0.1875 to 0.1875
Outputs:
- updated: bfloat16 [192, 512, 256], P('ha', 'wa')
Inputs may be any that keep to these rules, and one draw needn't show every extreme that they name: `blk_index`: two entries are equal exactly when their query and key positions differ by the same row and column offsets inside the window. `grid_index`: two entries are equal exactly when their query and key positions differ by the same row and column offsets inside the window.
All inputs are finite; a program needn't handle non-finite values.
Results may differ from a plain program's by a relative error of at most 0.013.
Values may be sent and summed in bfloat16 or wider, within the bound.
A program may use at most 128 MiB of HBM per device.

v0:
```python
import functools
import math

import jax
import jax.numpy as jnp
from jax import lax
from jax.experimental import pallas as pl
from jax.experimental.pallas import tpu as pltpu
from jax.sharding import PartitionSpec as P

EPS = 1e-05
HEADS = 8
SIDE = 8
TOKENS = SIDE * SIDE
GROUP = 16
LOG2E = math.log2(math.e)
MESH = pl.DeviceIdType.MESH
VMEM_LIMIT = 56 * 1024 * 1024


def halo(field):
    def shifted(x, axis):
        count = lax.axis_size(axis)
        up = [(i, i + 1) for i in range(count - 1)]
        down = [(j, i) for i, j in up]
        return up, down

    up, down = shifted(field, "ha")
    top = lax.ppermute(field[-1:], "ha", up)
    bottom = lax.ppermute(field[:1], "ha", down)
    tall = jnp.concatenate([top, field, bottom], axis=0)
    up, down = shifted(field, "wa")
    left = lax.ppermute(tall[:, -1], "wa", up)
    right = lax.ppermute(tall[:, 0], "wa", down)
    rows, cols, width = tall.shape
    inner = tall.reshape(rows, cols // SIDE, SIDE, width).transpose(0, 2, 1, 3)
    before = jnp.concatenate([left[:, None], inner[:, -1, :-1]], axis=1)
    after = jnp.concatenate([inner[:, 0, 1:], right[:, None]], axis=1)
    return jnp.concatenate([before[:, None], inner, after[:, None]], axis=1)


def norm(wide):
    center = wide - jnp.mean(wide, axis=-1, keepdims=True)
    spread = jnp.mean(center * center, axis=-1, keepdims=True)
    return (center * lax.rsqrt(spread + EPS)).astype(jnp.bfloat16)


def gelu(v):
    kind = v.dtype
    first = jnp.asarray(math.sqrt(2 / math.pi), kind)
    third = jnp.asarray(math.sqrt(2 / math.pi) * 0.044715, kind)
    half = jnp.asarray(0.5, kind) * v
    return half + half * jnp.tanh(v * (first + third * (v * v)))


def put(ref, rows, value):
    for c in range(value.shape[1] // 128):
        ref[c, rows, :] = value[:, c * 128 : (c + 1) * 128]


def get(ref, rows, first=0, last=None):
    last = ref.shape[0] if last is None else last
    return jnp.concatenate([ref[c, rows, :] for c in range(first, last)], axis=1)


def dot(a, b):
    return jnp.dot(a, b, preferred_element_type=jnp.float32)


def attention(x_s, qkv_s, mix_s, qkv_w, bias, mask):
    tiles, cells, lane = x_s.shape
    width = tiles * lane
    block = 256
    scale = LOG2E / math.sqrt(width // HEADS)

    def project(i, _):
        rows = pl.ds(pl.multiple_of(i * block, block), block)
        qkv = dot(norm(get(x_s, rows)), qkv_w[...])
        put(qkv_s, rows, jnp.concatenate([qkv[:, :width] * scale, qkv[:, width:]], axis=1))
        return 0

    lax.fori_loop(0, cells // block, project, 0)
    low = lax.broadcasted_iota(jnp.int32, (TOKENS, 2 * TOKENS), 1) < TOKENS

    def one(w):
        rows = pl.ds(w, TOKENS, stride=GROUP)
        q = get(qkv_s, rows, 0, tiles).astype(jnp.bfloat16)
        k = get(qkv_s, rows, tiles, 2 * tiles).astype(jnp.bfloat16)
        v = get(qkv_s, rows, 2 * tiles).astype(jnp.bfloat16)
        keys = jnp.concatenate([k] * HEADS, axis=0) * mask[...]
        vals = jnp.concatenate([v] * HEADS, axis=0) * mask[...]
        s = lax.dot_general(
            q, keys, (((1,), (1,)), ((), ())), preferred_element_type=jnp.float32
        )
        parts = []
        for c in range(HEADS // 2):
            lanes = slice(c * 2 * TOKENS, (c + 1) * 2 * TOKENS)
            part = s[:, lanes] + bias[:, lanes]
            one_max = jnp.max(jnp.where(low, part, -jnp.inf), axis=1, keepdims=True)
            two_max = jnp.max(jnp.where(low, -jnp.inf, part), axis=1, keepdims=True)
            parts.append(jnp.exp2(part - jnp.where(low, one_max, two_max)).astype(jnp.bfloat16))
        p = jnp.concatenate(parts, axis=1)
        put(mix_s, rows, dot(p, vals) / dot(p, mask[...]))

    def several(g, _):
        for w in range(4):
            one(g * 4 + w)
        return 0

    lax.fori_loop(0, GROUP // 4, several, 0)


def feed_forward(i, block, x_s, mix_s, out_w, up_w, down_w):
    rows = pl.ds(pl.multiple_of(i * block, block), block)
    x = get(x_s, rows) + dot(get(mix_s, rows).astype(jnp.bfloat16), out_w[...])
    x = x.astype(jnp.bfloat16).astype(jnp.float32)
    inner = gelu(dot(norm(x), up_w[...]).astype(jnp.bfloat16))
    return rows, x + dot(inner, down_w[...])


def convolve(k, field, expand_w, dw, project_w, hidden, act, x_s):
    width = field.shape[-1]
    channels = expand_w.shape[-1]
    span = SIDE + 2

    def expand(y, _):
        cells = field[k, y].reshape(span * GROUP, width).astype(jnp.float32)
        inner = gelu(dot(norm(cells), expand_w[...]).astype(jnp.bfloat16))
        hidden[y] = inner.reshape(span, GROUP, channels)
        return 0

    lax.fori_loop(0, span, expand, 0)

    def depthwise(y, _):
        for b in range(channels // 256):
            lanes = slice(b * 256, (b + 1) * 256)
            total = None
            for dy in range(3):
                for dx in range(3):
                    term = hidden[y + dy, dx : dx + SIDE, :, lanes] * dw[3 * dy + dx, :, lanes][None]
                    total = term if total is None else total + term
            act[:, lanes] = gelu(total).reshape(SIDE * GROUP, 256)
        center = field[k, y + 1, 1 : 1 + SIDE].reshape(SIDE * GROUP, width).astype(jnp.float32)
        x = center + dot(act[...], project_w[...])
        rows = pl.ds(pl.multiple_of(y * (SIDE * GROUP), SIDE * GROUP), SIDE * GROUP)
        put(x_s, rows, x.astype(jnp.bfloat16).astype(jnp.float32))
        return 0

    lax.fori_loop(0, SIDE, depthwise, 0)


def layer_kernel(
    lead, n_ha, n_wa, part_rows, part_cols,
    field, expand_w, dw, project_w, blk_qkv, blk_out, blk_bias, blk_up, blk_down,
    grid_qkv, grid_out, grid_bias, grid_up, grid_down, mask,
    out,
    hidden, act, x_s, qkv_s, mix_s, ready, arrived, result,
    send_go, recv_go, send_back, recv_back,
):
    chunks, devices, per, width = out.shape
    my_ha, my_wa = lax.axis_index("ha"), lax.axis_index("wa")
    me = my_ha * n_wa + my_wa
    blocks = SIDE // part_rows
    size = part_rows * SIDE * GROUP
    share = devices // blocks
    lines = part_rows * part_cols

    barrier = pltpu.get_barrier_semaphore()

    def greet(o, _):
        d = lax.rem(me + o, devices)
        pl.semaphore_signal(
            barrier, inc=1, device_id=(d // n_wa, lax.rem(d, n_wa)), device_id_type=MESH
        )
        return 0

    lax.fori_loop(1, devices, greet, 0)

    def ship(k, d, source, target, send_sem, recv_sem):
        @pl.when(d != me)
        def _():
            pltpu.make_async_remote_copy(
                src_ref=source.at[k, d],
                dst_ref=target.at[k, me],
                send_sem=send_sem.at[k],
                recv_sem=recv_sem.at[k],
                device_id=(d // n_wa, lax.rem(d, n_wa)),
                device_id_type=MESH,
            ).start()

        @pl.when(d == me)
        def _():
            target[k, d] = source[k, d]

    def all_of(k, source, target, send_sem, recv_sem):
        other = lax.rem(me + 1, devices)
        return pltpu.make_async_remote_copy(
            src_ref=source.at[k, pl.ds(0, devices - 1)],
            dst_ref=target.at[k, pl.ds(0, devices - 1)],
            send_sem=send_sem.at[k],
            recv_sem=recv_sem.at[k],
            device_id=(other // n_wa, lax.rem(other, n_wa)),
            device_id_type=MESH,
        )

    def block_chunk(k, _):
        convolve(k, field, expand_w, dw, project_w, hidden, act, x_s)
        attention(x_s, qkv_s, mix_s, blk_qkv, blk_bias, mask)

        @pl.when(k == 0)
        def _():
            pl.semaphore_wait(barrier, devices - 1)

        def step(n, _):
            i = lax.rem(n + my_ha + 1, blocks)
            rows, value = feed_forward(i, size, x_s, mix_s, blk_out, blk_up, blk_down)
            put(x_s, rows, value)
            for w in range(GROUP):
                strip, square = w // SIDE, w % SIDE
                for h in range(SIDE // part_cols):
                    first = h * part_cols * GROUP + w
                    piece = jnp.concatenate(
                        [
                            get(
                                x_s,
                                pl.ds(
                                    i * size + r * SIDE * GROUP + first, part_cols, stride=GROUP
                                ),
                            )
                            for r in range(part_rows)
                        ],
                        axis=0,
                    ).astype(jnp.bfloat16)
                    if lead == 2:
                        ready[k, i * n_wa + square, strip * lines : (strip + 1) * lines] = piece
                    else:
                        row = strip * blocks + i
                        ready[k, row * n_wa + square * (SIDE // part_cols) + h] = piece

            def go(o, _):
                d = lax.rem(my_wa + o, n_wa)
                for strip in range(2 // lead):
                    ship(
                        k, (strip * blocks + i) * n_wa + d, ready, arrived, send_go, recv_go
                    )
                return 0

            lax.fori_loop(0, n_wa, go, 0)
            return 0

        lax.fori_loop(0, blocks, step, 0)
        return 0

    lax.fori_loop(0, chunks, block_chunk, 0)

    def grid_chunk(k, _):
        all_of(k, ready, arrived, send_go, recv_go).wait_recv()
        put(x_s, slice(None), arrived[k].astype(jnp.float32).reshape(devices * per, width))
        attention(x_s, qkv_s, mix_s, grid_qkv, grid_bias, mask)

        def step(n, _):
            i = lax.rem(n + my_ha + 1, blocks)
            rows, value = feed_forward(i, size, x_s, mix_s, grid_out, grid_up, grid_down)
            first = pl.multiple_of(i * share, share)
            result[k, pl.ds(first, share)] = value.reshape(share, per, width).astype(jnp.bfloat16)

            def go(o, _):
                d = i * share + lax.rem(my_wa + o, share)
                ship(k, d, result, out, send_back, recv_back)
                return 0

            lax.fori_loop(0, share, go, 0)
            return 0

        lax.fori_loop(0, blocks, step, 0)
        return 0

    lax.fori_loop(0, chunks, grid_chunk, 0)

    def finish(k, _):
        all_of(k, ready, arrived, send_go, recv_go).wait_send()
        all_of(k, result, out, send_back, recv_back).wait()
        return 0

    lax.fori_loop(0, chunks, finish, 0)


def position_bias(table, index):
    buckets = table.shape[0]
    onehot = (index[:, :, None] == lax.broadcasted_iota(jnp.int32, (1, 1, buckets), 2)).astype(
        jnp.float32
    )
    bias = jnp.einsum("pqk,kh->phq", onehot, table * LOG2E, precision=lax.Precision.HIGHEST)
    return bias.reshape(index.shape[0], -1)


def on_device(
    field,
    expand_w,
    dw_kernel,
    project_w,
    blk_qkv,
    blk_out,
    blk_table,
    blk_index,
    blk_up,
    blk_down,
    grid_qkv,
    grid_out,
    grid_table,
    grid_index,
    grid_up,
    grid_down,
):
    rows, cols, width = field.shape
    channels = expand_w.shape[1]
    n_ha = lax.axis_size("ha")
    n_wa = lax.axis_size("wa")
    lead = SIDE // n_ha
    stride_rows = rows // lead
    chunks = rows // (2 * SIDE)
    chunk_rows = stride_rows // chunks
    part_rows = chunk_rows // n_ha
    part_cols = cols // n_wa
    strips = 2
    cells = GROUP * TOKENS

    blk_bias = position_bias(blk_table, blk_index)
    i = jnp.arange(n_ha)[:, None, None] * lead + jnp.arange(lead)[None, None, :]
    j = jnp.arange(SIDE)[None, :, None]
    order = (SIDE * i + j).reshape(-1)
    grid_bias = position_bias(grid_table, grid_index[order][:, order])
    mask = (
        (lax.broadcasted_iota(jnp.int32, (HEADS * TOKENS, width), 0) // TOKENS)
        == (lax.broadcasted_iota(jnp.int32, (HEADS * TOKENS, width), 1) // (width // HEADS))
    ).astype(jnp.bfloat16)
    dw = jnp.broadcast_to(dw_kernel.astype(jnp.bfloat16)[:, None], (9, GROUP, channels))

    framed = halo(field)
    per = cells // (n_ha * n_wa)
    starts = [
        (m // (strips // lead)) * stride_rows + (m % (strips // lead)) * SIDE
        for m in range(strips)
    ]
    strip = jnp.stack(
        [
            jnp.stack([framed[s + k * chunk_rows :][: SIDE + 2] for s in starts], axis=2)
            for k in range(chunks)
        ]
    ).reshape(chunks, SIDE + 2, SIDE + 2, GROUP, width)
    parts = (chunks, n_ha * n_wa, per, width)
    layer = pl.pallas_call(
        functools.partial(layer_kernel, lead, n_ha, n_wa, part_rows, part_cols),
        out_shape=jax.ShapeDtypeStruct(parts, jnp.bfloat16),
        in_specs=[pl.BlockSpec(memory_space=pltpu.VMEM)] * 15,
        out_specs=pl.BlockSpec(memory_space=pltpu.VMEM),
        scratch_shapes=[
            pltpu.VMEM((SIDE + 2, SIDE + 2, GROUP, channels), jnp.bfloat16),
            pltpu.VMEM((SIDE * GROUP, channels), jnp.bfloat16),
            pltpu.VMEM((width // 128, cells, 128), jnp.float32),
            pltpu.VMEM((3 * width // 128, cells, 128), jnp.float32),
            pltpu.VMEM((width // 128, cells, 128), jnp.float32),
            pltpu.VMEM(parts, jnp.bfloat16),
            pltpu.VMEM(parts, jnp.bfloat16),
            pltpu.VMEM(parts, jnp.bfloat16),
        ]
        + [pltpu.SemaphoreType.DMA((chunks,))] * 4,
        compiler_params=pltpu.CompilerParams(
            vmem_limit_bytes=VMEM_LIMIT, collective_id=0, has_side_effects=True
        ),
        cost_estimate=pl.CostEstimate(
            flops=2 * rows * cols * width * 36 * width, bytes_accessed=12 << 20, transcendentals=0
        ),
    )
    back = layer(
        strip, expand_w, dw, project_w, blk_qkv, blk_out, blk_bias, blk_up, blk_down,
        grid_qkv, grid_out, grid_bias, grid_up, grid_down, mask,
    )
    updated = back.reshape(chunks, n_ha, n_wa, lead, part_rows, part_cols, width)
    return updated.transpose(3, 0, 1, 4, 2, 5, 6).reshape(rows, cols, width)


def solution(mesh):
    placed = (P("ha", "wa", None),) + (P(),) * 15
    return jax.shard_map(
        on_device, mesh=mesh, in_specs=placed, out_specs=P("ha", "wa", None), check_vma=False
    )
```

profile of v0, /device:TPU:0, one launch (start us, length us, event | category | flops | bytes accessed | tf_op | source)
XLA Modules:
  0.0 146.6 jit_solution(17485368595049135592)
XLA Ops:
  0.0 0.0 copy-start
  0.0 0.0 copy-start.3
  0.0 0.0 copy-start.4
  0.0 0.0 copy-start.2
  0.0 2.3 %copy.28 = bf16[48,64,256]{2,0,1:T(8,128)(2,1)S(1)} copy(bf16[48,64,256]{2,1,0:T(8,128)(2,1)} %param.16) | data formatting | bytes 3145728 | tf_op args[0]
  2.3 0.1 fusion.19
  2.5 4.9 %collective-permute-start = (bf16[1,64,256]{2,0,1:T(2,128)(2,1)S(1)}, bf16[1,64,256]{2,0,1:T(2,128)(2,1)S(1)}, u32[]{:S(2)}, u32[]{:S(2)}) collective-permute-start(bf16[1,64,256]{2,0,1:T(2,128)(2,1)S(1)} %get-tuple-element.15), channel_id=1, source_target_pairs={{0,8},{8,16},{16,24},{1,9},{9,17},{17,25},{2,10},{10,18},{18,26},{... | collective-permute-start | bytes 98312 | tf_op jit(solution)/shard_map/ppermute | solution.py:29
  7.3 1.3 collective-permute-start.1
  8.7 0.1 add_multiply_fusion
  8.8 0.1 add.79
  8.9 0.0 copy-done
  8.9 0.0 copy-start.1
  8.9 0.6 gather_fusion
  9.5 0.1 copy.39
  9.6 0.6 gather_fusion.1
  10.2 0.1 copy.40
  10.3 0.0 copy-done.3
  10.3 3.2 %fusion.4 = f32[64,8,64]{2,1,0:T(8,128)S(1)} fusion(s32[64,64]{1,0:T(8,128)S(1)} %copy.40, f32[225,8]{0,1:T(8,128)S(1)} %copy-done.3), kind=kOutput, calls=%fused_computation.12 | convolution fusion | flops 89397000 | bytes 154656 | tf_op jit(solution)/shard_map/pqk,kh->phq/dot_general | solution.py:293
  13.5 0.0 copy-done.4
  13.5 0.0 copy-done.2
  13.5 3.2 %fusion.5 = f32[64,8,64]{2,1,0:T(8,128)S(1)} fusion(s32[64,64]{1,0:T(8,128)S(1)} %copy-done.2, f32[225,8]{0,1:T(8,128)S(1)} %copy-done.4), kind=kOutput, calls=%fused_computation.13 | convolution fusion | flops 89397000 | bytes 154656 | tf_op jit(solution)/shard_map/pqk,kh->phq/dot_general | solution.py:293
  16.7 1.0 fusion.6.mask
  17.7 0.8 reshape.86.grid_bias
  18.5 0.8 reshape.85.blk_bias
  19.2 0.0 copy-done.1
  19.2 0.0 collective-permute-done
  19.2 0.0 collective-permute-done.1
  19.3 1.2 pad_maximum_fusion.2
  20.4 0.9 copy.46
  21.4 1.5 collective-permute-start.2
  22.8 1.5 %collective-permute-start.3 = (bf16[50,256]{1,0:T(8,128)(2,1)S(1)}, bf16[50,256]{1,0:T(8,128)(2,1)S(1)}, u32[]{:S(2)}, u32[]{:S(2)}) collective-permute-start(bf16[50,256]{1,0:T(8,128)(2,1)S(1)} %get-tuple-element.12), channel_id=1, source_target_pairs={{1,0},{2,1},{3,2},{4,3},{5,4},{6,5},{7,6},{9,8},{10,9},{11,10},{12... | collective-permute-start | bytes 76808 | tf_op jit(solution)/shard_map/ppermute | solution.py:34
  24.3 0.1 slice_bitcast_fusion.7
  24.4 0.9 copy.35
  25.3 0.0 collective-permute-done.2
  25.3 2.2 %collective-permute-done.3 = bf16[50,256]{1,0:T(8,128)(2,1)S(1)} collective-permute-done((bf16[50,256]{1,0:T(8,128)(2,1)S(1)}, bf16[50,256]{1,0:T(8,128)(2,1)S(1)}, u32[]{:S(2)}, u32[]{:S(2)}) %collective-permute-start.3) | collective-permute-done | bytes 25632 | tf_op jit(solution)/shard_map/ppermute | solution.py:34
  27.6 0.2 maximum_bitcast_fusion.1
  27.8 0.2 pad_maximum_fusion.1
  28.1 0.2 slice_bitcast_fusion.5
  28.3 0.1 copy_bitcast_fusion.2
  28.4 0.1 copy_bitcast_fusion.1
  28.5 0.1 maximum_bitcast_fusion
  28.6 1.7 %pad_maximum_fusion.field = bf16[3,10,10,16,256]{4,3,2,1,0:T(8,128)(2,1)} fusion(bf16[1,10,10,16,256]{4,3,2,1,0:T(8,128)(2,1)S(1)} %maximum_bitcast_fusion, bf16[1,10,10,16,256]{4,3,2,1,0:T(8,128)(2,1)S(1)} %copy_bitcast_fusion.1, bf16[1,10,10,16,256]{4,3,2,1,0:T(8,128)(2,1)S(1)} %copy_bitcast_fusion.2), kind=kLoop, calls=%fused_computation.6 | loop fusion | flops 2457600 | bytes 4915200 | tf_op jit(solution)/shard_map/stack | solution.py:345
  30.3 0.7 broadcast_in_dim.14.dw
  31.0 112.8 %shard_map.154 = bf16[3,32,32,256]{3,2,1,0:T(8,128)(2,1)} custom-call(bf16[3,10,10,16,256]{4,3,2,1,0:T(8,128)(2,1)} %pad_maximum_fusion.field, bf16[256,1024]{1,0:T(8,128)(2,1)} %expand_w.1, bf16[9,16,1024]{2,1,0:T(8,128)(2,1)} %broadcast_in_dim.14.dw, bf16[1024,256]{1,0:T(8,128)(2,1)} %project_w.1, bf16[256,768]{1,0:T(8,128)(2,1)} %blk_qkv.1, ...), custom_call_target="tpu_custom_call" | custom-call | flops 14495514624 | bytes 12582912 | tf_op jit(solution)/shard_map/pallas_call | solution.py:375
  143.8 2.8 %copy.41 = bf16[2,3,4,2,8,8,256]{6,5,4,3,2,1,0:T(8,128)(2,1)} copy(bf16[2,3,4,2,8,8,256]{6,5,3,0,4,2,1:T(8,128)(2,1)} %bitcast.62) | data formatting | bytes 3145728 | tf_op jit(solution)/shard_map/transpose | solution.py:380
  (12 shorter events, 0.1 us)
Async XLA Ops:
  0.0 8.9 %copy-start = (s32[64,64]{1,0:T(8,128)S(1)}, s32[64,64]{1,0:T(8,128)}, u32[]{:S(2)}) copy-start(s32[64,64]{1,0:T(8,128)} %param.29) | copy-start | bytes 49156
  0.0 10.3 %copy-start.3 = (f32[225,8]{0,1:T(8,128)S(1)}, f32[225,8]{0,1:T(8,128)}, u32[]{:S(2)}) copy-start(f32[225,8]{0,1:T(8,128)} %param.28) | copy-start | bytes 21604
  0.0 13.5 %copy-start.4 = (f32[225,8]{0,1:T(8,128)S(1)}, f32[225,8]{0,1:T(8,128)}, u32[]{:S(2)}) copy-start(f32[225,8]{0,1:T(8,128)} %param.22) | copy-start | bytes 21604
  0.0 13.5 %copy-start.2 = (s32[64,64]{1,0:T(8,128)S(1)}, s32[64,64]{1,0:T(8,128)}, u32[]{:S(2)}) copy-start(s32[64,64]{1,0:T(8,128)} %param.23) | copy-start | bytes 49156
  2.5 16.8 %collective-permute-start = (bf16[1,64,256]{2,0,1:T(2,128)(2,1)S(1)}, bf16[1,64,256]{2,0,1:T(2,128)(2,1)S(1)}, u32[]{:S(2)}, u32[]{:S(2)}) collective-permute-start(bf16[1,64,256]{2,0,1:T(2,128)(2,1)S(1)} %get-tuple-element.15), channel_id=1, source_target_pairs={{0,8},{8,16},{16,24},{1,9},{9,17},{17,25},{2,10},{10,18},{18,26},{... | collective-permute-start | bytes 98312 | tf_op jit(solution)/shard_map/ppermute | solution.py:29
  7.3 11.9 %collective-permute-start.1 = (bf16[1,64,256]{2,0,1:T(2,128)(2,1)S(1)}, bf16[1,64,256]{2,0,1:T(2,128)(2,1)S(1)}, u32[]{:S(2)}, u32[]{:S(2)}) collective-permute-start(bf16[1,64,256]{2,0,1:T(2,128)(2,1)S(1)} %get-tuple-element.16), channel_id=1, source_target_pairs={{8,0},{16,8},{24,16},{9,1},{17,9},{25,17},{10,2},{18,10},{26,18},{... | collective-permute-start | bytes 98312 | tf_op jit(solution)/shard_map/ppermute | solution.py:30
  8.9 10.3 %copy-start.1 = (f32[9,1024]{1,0:T(8,128)S(1)}, f32[9,1024]{1,0:T(8,128)}, u32[]{:S(2)}) copy-start(f32[9,1024]{1,0:T(8,128)} %param.18) | copy-start | bytes 110596
  21.4 3.9 %collective-permute-start.2 = (bf16[50,256]{1,0:T(8,128)(2,1)S(1)}, bf16[50,256]{1,0:T(8,128)(2,1)S(1)}, u32[]{:S(2)}, u32[]{:S(2)}) collective-permute-start(bf16[50,256]{1,0:T(8,128)(2,1)S(1)} %get-tuple-element.11), channel_id=1, source_target_pairs={{0,1},{1,2},{2,3},{3,4},{4,5},{5,6},{6,7},{8,9},{9,10},{10,11},{11... | collective-permute-start | bytes 76808 | tf_op jit(solution)/shard_map/ppermute | solution.py:33
  22.8 4.7 %collective-permute-start.3 = (bf16[50,256]{1,0:T(8,128)(2,1)S(1)}, bf16[50,256]{1,0:T(8,128)(2,1)S(1)}, u32[]{:S(2)}, u32[]{:S(2)}) collective-permute-start(bf16[50,256]{1,0:T(8,128)(2,1)S(1)} %get-tuple-element.12), channel_id=1, source_target_pairs={{1,0},{2,1},{3,2},{4,3},{5,4},{6,5},{7,6},{9,8},{10,9},{11,10},{12... | collective-permute-start | bytes 76808 | tf_op jit(solution)/shard_map/ppermute | solution.py:34
where the time goes:
time: 147 us
  Pallas kernels  113 us (77%)
  local copies, waits for them, and re-layouts  11.2 us (8%)
  starting transfers between devices  9.08 us (6%)
  matrix products  6.42 us (4%)
  other arithmetic  4.67 us (3%)
  waiting for transfers between devices  2.22 us (2%)
    pallas_call x1, Pallas kernels, on_device(): layer(strip, expand_w, dw, project_w, blk_qkv, blk_out, blk_bias, blk_up,...  113 us
    dot_general x2, matrix products, position_bias(): jnp.einsum('pqk,kh->phq', onehot, table * LOG2E, precision=lax.Precision....  6.42 us
    ppermute x1, starting transfers between devices, halo(): top = lax.ppermute(field[-1:], 'ha', up)  4.85 us
  transfers between devices with their start and end apart: 4, of which 1 were waited for; matrix products, arithmetic and copies ran while one was open for 8% of the time, Pallas kernels for 0%

commit v1 on v0

--- a/solution.py
+++ b/solution.py
@@ -18,27 +18,6 @@
 VMEM_LIMIT = 56 * 1024 * 1024
 
 
-def halo(field):
-    def shifted(x, axis):
-        count = lax.axis_size(axis)
-        up = [(i, i + 1) for i in range(count - 1)]
-        down = [(j, i) for i, j in up]
-        return up, down
-
-    up, down = shifted(field, "ha")
-    top = lax.ppermute(field[-1:], "ha", up)
-    bottom = lax.ppermute(field[:1], "ha", down)
-    tall = jnp.concatenate([top, field, bottom], axis=0)
-    up, down = shifted(field, "wa")
-    left = lax.ppermute(tall[:, -1], "wa", up)
-    right = lax.ppermute(tall[:, 0], "wa", down)
-    rows, cols, width = tall.shape
-    inner = tall.reshape(rows, cols // SIDE, SIDE, width).transpose(0, 2, 1, 3)
-    before = jnp.concatenate([left[:, None], inner[:, -1, :-1]], axis=1)
-    after = jnp.concatenate([inner[:, 0, 1:], right[:, None]], axis=1)
-    return jnp.concatenate([before[:, None], inner, after[:, None]], axis=1)
-
-
 def norm(wide):
     center = wide - jnp.mean(wide, axis=-1, keepdims=True)
     spread = jnp.mean(center * center, axis=-1, keepdims=True)
@@ -70,7 +49,7 @@
 def attention(x_s, qkv_s, mix_s, qkv_w, bias, mask):
     tiles, cells, lane = x_s.shape
     width = tiles * lane
-    block = 256
+    block = 512
     scale = LOG2E / math.sqrt(width // HEADS)
 
     def project(i, _):
@@ -81,33 +60,37 @@
 
     lax.fori_loop(0, cells // block, project, 0)
     low = lax.broadcasted_iota(jnp.int32, (TOKENS, 2 * TOKENS), 1) < TOKENS
-
-    def one(w):
+    several = HEADS // tiles
+
+    def one(w, g):
         rows = pl.ds(w, TOKENS, stride=GROUP)
-        q = get(qkv_s, rows, 0, tiles).astype(jnp.bfloat16)
-        k = get(qkv_s, rows, tiles, 2 * tiles).astype(jnp.bfloat16)
-        v = get(qkv_s, rows, 2 * tiles).astype(jnp.bfloat16)
-        keys = jnp.concatenate([k] * HEADS, axis=0) * mask[...]
-        vals = jnp.concatenate([v] * HEADS, axis=0) * mask[...]
+        q = qkv_s[g, rows, :].astype(jnp.bfloat16)
+        k = qkv_s[tiles + g, rows, :].astype(jnp.bfloat16)
+        v = qkv_s[2 * tiles + g, rows, :].astype(jnp.bfloat16)
+        keys = jnp.concatenate([k] * several, axis=0) * mask[...]
+        vals = jnp.concatenate([v] * several, axis=0) * mask[...]
         s = lax.dot_general(
             q, keys, (((1,), (1,)), ((), ())), preferred_element_type=jnp.float32
         )
         parts = []
-        for c in range(HEADS // 2):
+        for c in range(several // 2):
             lanes = slice(c * 2 * TOKENS, (c + 1) * 2 * TOKENS)
-            part = s[:, lanes] + bias[:, lanes]
+            start = (g * several // 2 + c) * 2 * TOKENS
+            part = s[:, lanes] + bias[:, start : start + 2 * TOKENS]
             one_max = jnp.max(jnp.where(low, part, -jnp.inf), axis=1, keepdims=True)
             two_max = jnp.max(jnp.where(low, -jnp.inf, part), axis=1, keepdims=True)
             parts.append(jnp.exp2(part - jnp.where(low, one_max, two_max)).astype(jnp.bfloat16))
         p = jnp.concatenate(parts, axis=1)
-        put(mix_s, rows, dot(p, vals) / dot(p, mask[...]))
-
-    def several(g, _):
+        both = dot(p, jnp.concatenate([vals, mask[...]], axis=1))
+        mix_s[g, rows, :] = both[:, :lane] / both[:, lane:]
+
+    def step(n, _):
         for w in range(4):
-            one(g * 4 + w)
-        return 0
-
-    lax.fori_loop(0, GROUP // 4, several, 0)
+            for g in range(tiles):
+                one(n * 4 + w, g)
+        return 0
+
+    lax.fori_loop(0, GROUP // 4, step, 0)
 
 
 def feed_forward(i, block, x_s, mix_s, out_w, up_w, down_w):
@@ -118,42 +101,92 @@
     return rows, x + dot(inner, down_w[...])
 
 
-def convolve(k, field, expand_w, dw, project_w, hidden, act, x_s):
-    width = field.shape[-1]
+def neighbours():
+    return [(dy, dx) for dy in (-1, 0, 1) for dx in (-1, 0, 1) if dy or dx]
+
+
+def borders(n_ha, n_wa, field, stage, edge, rows_in, cols_in, corners_in, send_sem, recv_sem):
+    rows, cols, _ = field.shape
+    my_ha, my_wa = lax.axis_index("ha"), lax.axis_index("wa")
+    result = []
+    for n, (dy, dx) in enumerate(neighbours()):
+        there = (my_ha + dy, my_wa + dx)
+        exists = (there[0] >= 0) & (there[0] < n_ha) & (there[1] >= 0) & (there[1] < n_wa)
+        from_ha, from_wa = my_ha - dy, my_wa - dx
+        comes = (from_ha >= 0) & (from_ha < n_ha) & (from_wa >= 0) & (from_wa < n_wa)
+        row = 0 if dy < 0 else rows - 1
+        low, left = int(dy < 0), int(dx < 0)
+        if dx == 0:
+            source, target = field.at[row], rows_in.at[low]
+        elif dy == 0:
+            source, target = edge.at[1 - left], cols_in.at[left]
+        else:
+            first = 0 if dx < 0 else cols - GROUP
+            source, target = field.at[row, pl.ds(first, GROUP)], corners_in.at[2 * low + left]
+        copy = pltpu.make_async_remote_copy(
+            src_ref=source,
+            dst_ref=target,
+            send_sem=send_sem.at[n],
+            recv_sem=recv_sem.at[n],
+            device_id=there,
+            device_id_type=MESH,
+        )
+        result.append((copy, exists, comes, target))
+    return result
+
+
+def convolve(k, starts, chunk_rows, pitch, stage, expand_w, dw, project_w, hidden, act, x_s):
     channels = expand_w.shape[-1]
     span = SIDE + 2
 
-    def expand(y, _):
-        cells = field[k, y].reshape(span * GROUP, width).astype(jnp.float32)
+    def row(y, first, last):
+        pieces = []
+        for t in range(first, last):
+            for start in starts:
+                at = (start + k * chunk_rows + y) * pitch + SIDE - 1 + t
+                pieces.append(get(stage, pl.ds(at, SIDE, stride=SIDE)))
+        return pieces
+
+    def expand(n, _):
+        cells = jnp.concatenate(row(2 * n, 0, span) + row(2 * n + 1, 0, span), axis=0)
         inner = gelu(dot(norm(cells), expand_w[...]).astype(jnp.bfloat16))
-        hidden[y] = inner.reshape(span, GROUP, channels)
-        return 0
-
-    lax.fori_loop(0, span, expand, 0)
-
-    def depthwise(y, _):
-        for b in range(channels // 256):
-            lanes = slice(b * 256, (b + 1) * 256)
-            total = None
-            for dy in range(3):
-                for dx in range(3):
-                    term = hidden[y + dy, dx : dx + SIDE, :, lanes] * dw[3 * dy + dx, :, lanes][None]
-                    total = term if total is None else total + term
-            act[:, lanes] = gelu(total).reshape(SIDE * GROUP, 256)
-        center = field[k, y + 1, 1 : 1 + SIDE].reshape(SIDE * GROUP, width).astype(jnp.float32)
+        hidden[pl.ds(2 * n, 2)] = inner.reshape(2, span, GROUP, channels)
+        return 0
+
+    lax.fori_loop(0, span // 2, expand, 0)
+    size = SIDE * GROUP
+
+    def depthwise(n, _):
+        for half in range(2):
+            y = 2 * n + half
+            for b in range(channels // 256):
+                lanes = slice(b * 256, (b + 1) * 256)
+                total = None
+                for dy in range(3):
+                    for dx in range(3):
+                        term = (
+                            hidden[y + dy, dx : dx + SIDE, :, lanes]
+                            * dw[3 * dy + dx, :, lanes][None]
+                        )
+                        total = term if total is None else total + term
+                act[half * size : (half + 1) * size, lanes] = gelu(total).reshape(size, 256)
+        center = jnp.concatenate(
+            row(2 * n + 1, 1, 1 + SIDE) + row(2 * n + 2, 1, 1 + SIDE), axis=0
+        )
         x = center + dot(act[...], project_w[...])
-        rows = pl.ds(pl.multiple_of(y * (SIDE * GROUP), SIDE * GROUP), SIDE * GROUP)
+        rows = pl.ds(pl.multiple_of(n * (2 * size), 2 * size), 2 * size)
         put(x_s, rows, x.astype(jnp.bfloat16).astype(jnp.float32))
         return 0
 
-    lax.fori_loop(0, SIDE, depthwise, 0)
+    lax.fori_loop(0, SIDE // 2, depthwise, 0)
 
 
 def layer_kernel(
-    lead, n_ha, n_wa, part_rows, part_cols,
-    field, expand_w, dw, project_w, blk_qkv, blk_out, blk_bias, blk_up, blk_down,
-    grid_qkv, grid_out, grid_bias, grid_up, grid_down, mask,
+    lead, n_ha, n_wa, part_rows, part_cols, starts, chunk_rows,
+    field, expand_w, dw_kernel, project_w, blk_qkv, blk_out, blk_bias, blk_up, blk_down,
+    grid_qkv, grid_out, grid_bias, grid_up, grid_down,
     out,
+    stage, edge, rows_in, cols_in, corners_in, mask, dw, edge_send, edge_recv,
     hidden, act, x_s, qkv_s, mix_s, ready, arrived, result,
     send_go, recv_go, send_back, recv_back,
 ):
@@ -175,6 +208,48 @@
         return 0
 
     lax.fori_loop(1, devices, greet, 0)
+
+    rows, cols, _ = field.shape
+    pitch = cols + 2 * SIDE
+
+    def lay(y, _):
+        at = pl.ds(pl.multiple_of((y + 1) * pitch + SIDE, SIDE), cols)
+        put(stage, at, field[y].astype(jnp.float32))
+        return 0
+
+    lax.fori_loop(0, rows, lay, 0)
+    edge[0] = get(stage, pl.ds(pitch + SIDE, rows, stride=pitch)).astype(jnp.bfloat16)
+    edge[1] = get(stage, pl.ds(pitch + SIDE + cols - 1, rows, stride=pitch)).astype(jnp.bfloat16)
+    pl.semaphore_wait(barrier, devices - 1)
+    crossings = borders(
+        n_ha, n_wa, field, stage, edge, rows_in, cols_in, corners_in, edge_send, edge_recv
+    )
+    for copy, exists, _, _ in crossings:
+        pl.when(exists)(copy.start)
+    mask[...] = (
+        (lax.broadcasted_iota(jnp.int32, mask.shape, 0) // TOKENS)
+        == (lax.broadcasted_iota(jnp.int32, mask.shape, 1) // (width // HEADS))
+    ).astype(jnp.float32).astype(jnp.bfloat16)
+    for tap in range(9):
+        dw[tap] = jnp.broadcast_to(dw_kernel[tap : tap + 1, :], dw.shape[1:]).astype(jnp.bfloat16)
+    for copy, exists, comes, target in crossings:
+        @pl.when(jnp.logical_not(comes))
+        def _():
+            target[...] = jnp.zeros(target.shape, jnp.bfloat16)
+
+        pl.when(comes)(copy.wait_recv)
+        pl.when(exists)(copy.wait_send)
+    bottom = (rows + 1) * pitch
+    put(stage, slice(SIDE, SIDE + cols), rows_in[0].astype(jnp.float32))
+    put(stage, slice(bottom + SIDE, bottom + SIDE + cols), rows_in[1].astype(jnp.float32))
+    left, right = SIDE - 1, SIDE + cols
+    put(stage, pl.ds(pitch + left, rows, stride=pitch), cols_in[0].astype(jnp.float32))
+    put(stage, pl.ds(pitch + right, rows, stride=pitch), cols_in[1].astype(jnp.float32))
+    for n, (at, line) in enumerate(
+        [(left, GROUP - 1), (right, 0), (bottom + left, GROUP - 1), (bottom + right, 0)]
+    ):
+        cell = corners_in[n].astype(jnp.float32)[line : line + 1]
+        put(stage, slice(at, at + 1), cell)
 
     def ship(k, d, source, target, send_sem, recv_sem):
         @pl.when(d != me)
@@ -204,12 +279,10 @@
         )
 
     def block_chunk(k, _):
-        convolve(k, field, expand_w, dw, project_w, hidden, act, x_s)
+        convolve(
+            k, starts, chunk_rows, pitch, stage, expand_w, dw, project_w, hidden, act, x_s
+        )
         attention(x_s, qkv_s, mix_s, blk_qkv, blk_bias, mask)
-
-        @pl.when(k == 0)
-        def _():
-            pl.semaphore_wait(barrier, devices - 1)
 
         def step(n, _):
             i = lax.rem(n + my_ha + 1, blocks)
@@ -285,13 +358,28 @@
     lax.fori_loop(0, chunks, finish, 0)
 
 
-def position_bias(table, index):
-    buckets = table.shape[0]
-    onehot = (index[:, :, None] == lax.broadcasted_iota(jnp.int32, (1, 1, buckets), 2)).astype(
-        jnp.float32
-    )
-    bias = jnp.einsum("pqk,kh->phq", onehot, table * LOG2E, precision=lax.Precision.HIGHEST)
-    return bias.reshape(index.shape[0], -1)
+def bias_kernel(tables, indices, *outs):
+    low = lax.broadcasted_iota(jnp.int32, (TOKENS, 2 * TOKENS), 1) < TOKENS
+    for a in range(2):
+        index = jnp.concatenate([indices[a], indices[a]], axis=1)
+        within = index % 128
+        upper = index >= 128
+        found = []
+        for h in range(HEADS):
+            halves = [
+                jnp.take_along_axis(
+                    jnp.broadcast_to(tables[a, h : h + 1, n * 128 : (n + 1) * 128], index.shape),
+                    within,
+                    axis=1,
+                    mode="promise_in_bounds",
+                )
+                for n in range(2)
+            ]
+            found.append(jnp.where(upper, halves[1], halves[0]))
+        for c in range(HEADS // 2):
+            outs[a][:, c * 2 * TOKENS : (c + 1) * 2 * TOKENS] = (
+                jnp.where(low, found[2 * c], found[2 * c + 1]) * LOG2E
+            )
 
 
 def on_device(
@@ -325,38 +413,40 @@
     strips = 2
     cells = GROUP * TOKENS
 
-    blk_bias = position_bias(blk_table, blk_index)
-    i = jnp.arange(n_ha)[:, None, None] * lead + jnp.arange(lead)[None, None, :]
-    j = jnp.arange(SIDE)[None, :, None]
-    order = (SIDE * i + j).reshape(-1)
-    grid_bias = position_bias(grid_table, grid_index[order][:, order])
-    mask = (
-        (lax.broadcasted_iota(jnp.int32, (HEADS * TOKENS, width), 0) // TOKENS)
-        == (lax.broadcasted_iota(jnp.int32, (HEADS * TOKENS, width), 1) // (width // HEADS))
-    ).astype(jnp.bfloat16)
-    dw = jnp.broadcast_to(dw_kernel.astype(jnp.bfloat16)[:, None], (9, GROUP, channels))
-
-    framed = halo(field)
+    ordered = grid_index.reshape(n_ha, lead, SIDE, n_ha, lead, SIDE).transpose(0, 2, 1, 3, 5, 4)
+    indices = jnp.stack([blk_index, ordered.reshape(TOKENS, TOKENS)])
+    tables = jnp.stack([blk_table, grid_table]).transpose(0, 2, 1)
+    tables = jnp.pad(tables, ((0, 0), (0, 0), (0, 256 - tables.shape[2])))
+    bias = pl.pallas_call(
+        bias_kernel,
+        out_shape=[jax.ShapeDtypeStruct((TOKENS, HEADS * TOKENS), jnp.float32)] * 2,
+    )(tables, indices)
     per = cells // (n_ha * n_wa)
     starts = [
         (m // (strips // lead)) * stride_rows + (m % (strips // lead)) * SIDE
         for m in range(strips)
     ]
-    strip = jnp.stack(
-        [
-            jnp.stack([framed[s + k * chunk_rows :][: SIDE + 2] for s in starts], axis=2)
-            for k in range(chunks)
-        ]
-    ).reshape(chunks, SIDE + 2, SIDE + 2, GROUP, width)
+    pitch = cols + 2 * SIDE
     parts = (chunks, n_ha * n_wa, per, width)
     layer = pl.pallas_call(
-        functools.partial(layer_kernel, lead, n_ha, n_wa, part_rows, part_cols),
+        functools.partial(
+            layer_kernel, lead, n_ha, n_wa, part_rows, part_cols, starts, chunk_rows
+        ),
         out_shape=jax.ShapeDtypeStruct(parts, jnp.bfloat16),
-        in_specs=[pl.BlockSpec(memory_space=pltpu.VMEM)] * 15,
+        in_specs=[pl.BlockSpec(memory_space=pltpu.VMEM)] * 14,
         out_specs=pl.BlockSpec(memory_space=pltpu.VMEM),
         scratch_shapes=[
+            pltpu.VMEM((width // 128, (rows + 2) * pitch, 128), jnp.float32),
+            pltpu.VMEM((2, rows, width), jnp.bfloat16),
+            pltpu.VMEM((2, cols, width), jnp.bfloat16),
+            pltpu.VMEM((2, rows, width), jnp.bfloat16),
+            pltpu.VMEM((4, GROUP, width), jnp.bfloat16),
+            pltpu.VMEM((HEADS * TOKENS * 128 // width, 128), jnp.bfloat16),
+            pltpu.VMEM((9, GROUP, channels), jnp.bfloat16),
+            pltpu.SemaphoreType.DMA((8,)),
+            pltpu.SemaphoreType.DMA((8,)),
             pltpu.VMEM((SIDE + 2, SIDE + 2, GROUP, channels), jnp.bfloat16),
-            pltpu.VMEM((SIDE * GROUP, channels), jnp.bfloat16),
+            pltpu.VMEM((2 * SIDE * GROUP, channels), jnp.bfloat16),
             pltpu.VMEM((width // 128, cells, 128), jnp.float32),
             pltpu.VMEM((3 * width // 128, cells, 128), jnp.float32),
             pltpu.VMEM((width // 128, cells, 128), jnp.float32),
@@ -373,8 +463,8 @@
         ),
     )
     back = layer(
-        strip, expand_w, dw, project_w, blk_qkv, blk_out, blk_bias, blk_up, blk_down,
-        grid_qkv, grid_out, grid_bias, grid_up, grid_down, mask,
+        field, expand_w, dw_kernel, project_w, blk_qkv, blk_out, bias[0], blk_up, blk_down,
+        grid_qkv, grid_out, bias[1], grid_up, grid_down,
     )
     updated = back.reshape(chunks, n_ha, n_wa, lead, part_rows, part_cols, width)
     return updated.transpose(3, 0, 1, 4, 2, 5, 6).reshape(rows, cols, width)

time: 147 us -> 109 us (0.74)
  Pallas kernels: 113 us -> 101 us
  starting transfers between devices: 9.08 us -> 0 us
  matrix products: 6.42 us -> 0 us
  local copies, waits for them, and re-layouts: 11.2 us -> 6.7 us
  other arithmetic: 4.67 us -> 1.34 us
  waiting for transfers between devices: 2.22 us -> 0 us
    pallas_call x1 -> x2, Pallas kernels: 113 us -> 101 us  [the longest x1 98.5 us: on_device(): layer(field, expand_w, dw_kernel, project_w, blk_qkv, blk_out, bias[0], b...]
    ppermute x4 -> x0, starting transfers between devices: 9.08 us -> none  [the longest x1 4.85 us: halo(): top = lax.ppermute(field[-1:], 'ha', up)]
    dot_general x2 -> x0, matrix products: 6.42 us -> none  [position_bias(): jnp.einsum('pqk,kh->phq', onehot, table * LOG2E, precision=lax.Precision....]
    unnamed x11 -> x2, local copies, waits for them, and re-layouts: 2.35 us -> 0.01 us
    ppermute x4 -> x0, waiting for transfers between devices: 2.22 us -> none  [the longest x1 2.21 us: halo(): right = lax.ppermute(tall[:, 0], 'wa', down)]
  transfers between devices with their start and end apart: 4 -> 0, of which waited for: 1 -> 0; matrix products, arithmetic and copies ran while one was open for 8% -> 0% of each run, Pallas kernels for 0% -> 0%
where the time goes in v1:
time: 109 us
  Pallas kernels  101 us (93%)
  local copies, waits for them, and re-layouts  6.7 us (6%)
  other arithmetic  1.34 us (1%)
    pallas_call x1, Pallas kernels, on_device(): layer(field, expand_w, dw_kernel, project_w, blk_qkv, blk_out, bias[0], b...  98.5 us
    transpose x1, local copies, waits for them, and re-layouts, on_device(): return updated.transpose(3, 0, 1, 4, 2, 5, 6).reshape(rows, cols, width)  2.76 us
    reshape x2, local copies, waits for them, and re-layouts, on_device(): grid_index.reshape(n_ha, lead, SIDE, n_ha, lead, SIDE)  2.69 us
    pallas_call x1, Pallas kernels, on_device(): pl.pallas_call(bias_kernel, out_shape=[jax.ShapeDtypeStruct((TOKENS, HEAD...  2.45 us

profile of v1, /device:TPU:0, one launch (start us, length us, event | category | flops | bytes accessed | tf_op | source)
XLA Modules:
  0.0 109.0 jit_solution(14641945429555675726)
XLA Ops:
  0.0 0.0 copy-start
  0.0 0.7 maximum_bitcast_fusion
  0.7 0.6 pad.4.tables
  1.3 1.1 %reshape.9 = s32[4,2,8,4,2,8]{5,4,3,2,1,0:T(2,128)S(1)} reshape(s32[64,64]{1,0:T(8,128)} %param.29) | data formatting | bytes 32768 | tf_op jit(solution)/shard_map/reshape | solution.py:416
  2.5 1.6 %copy.19 = s32[4,2,8,4,2,8]{4,5,3,1,2,0:T(8,128)S(1)} copy(s32[4,2,8,4,2,8]{5,4,3,2,1,0:T(2,128)S(1)} %reshape.9) | data formatting | bytes 32768 | tf_op jit(solution)/shard_map/reshape | solution.py:416
  4.0 0.6 stack_reshape.3
  4.7 0.0 copy-done
  4.7 0.6 pad_add_fusion.indices
  5.3 2.4 %shard_map.154 = (f32[64,512]{1,0:T(8,128)}, f32[64,512]{1,0:T(8,128)}) custom-call(f32[2,8,256]{2,1,0:T(8,128)} %pad.4.tables, s32[2,64,64]{2,1,0:T(8,128)} %pad_add_fusion.indices), custom_call_target="tpu_custom_call" | custom-call | tf_op jit(solution)/shard_map/pallas_call | solution.py:420
  7.7 98.5 %shard_map.155 = bf16[3,32,32,256]{3,2,1,0:T(8,128)(2,1)} custom-call(bf16[48,64,256]{2,1,0:T(8,128)(2,1)} %field.1, bf16[256,1024]{1,0:T(8,128)(2,1)} %expand_w.1, f32[9,1024]{1,0:T(8,128)} %dw_kernel.1, bf16[1024,256]{1,0:T(8,128)(2,1)} %project_w.1, bf16[256,768]{1,0:T(8,128)(2,1)} %blk_qkv.1, bf16[256,256]{1,0:T(8,128)(2,1)} %blk_out.1, ...), custom_call_target="tpu_custom_call" | custom-call | flops 14495514624 | bytes 12582912 | tf_op jit(solution)/shard_map/pallas_call | solution.py:465
  106.3 2.8 %copy.20 = bf16[2,3,4,2,8,8,256]{6,5,4,3,2,1,0:T(8,128)(2,1)} copy(bf16[2,3,4,2,8,8,256]{6,5,3,0,4,2,1:T(8,128)(2,1)} %bitcast.13) | data formatting | bytes 3145728 | tf_op jit(solution)/shard_map/transpose | solution.py:470
Async XLA Ops:
  0.0 4.7 %copy-start = (s32[64,64]{1,0:T(8,128)S(1)}, s32[64,64]{1,0:T(8,128)}, u32[]{:S(2)}) copy-start(s32[64,64]{1,0:T(8,128)} %param.23) | copy-start | bytes 49156

commit v2 on v1

--- a/solution.py
+++ b/solution.py
@@ -62,16 +62,16 @@
     low = lax.broadcasted_iota(jnp.int32, (TOKENS, 2 * TOKENS), 1) < TOKENS
     several = HEADS // tiles
 
-    def one(w, g):
+    def scores(w, g):
         rows = pl.ds(w, TOKENS, stride=GROUP)
         q = qkv_s[g, rows, :].astype(jnp.bfloat16)
         k = qkv_s[tiles + g, rows, :].astype(jnp.bfloat16)
-        v = qkv_s[2 * tiles + g, rows, :].astype(jnp.bfloat16)
         keys = jnp.concatenate([k] * several, axis=0) * mask[...]
-        vals = jnp.concatenate([v] * several, axis=0) * mask[...]
-        s = lax.dot_general(
+        return lax.dot_general(
             q, keys, (((1,), (1,)), ((), ())), preferred_element_type=jnp.float32
         )
+
+    def weights(s, g):
         parts = []
         for c in range(several // 2):
             lanes = slice(c * 2 * TOKENS, (c + 1) * 2 * TOKENS)
@@ -80,25 +80,43 @@
             one_max = jnp.max(jnp.where(low, part, -jnp.inf), axis=1, keepdims=True)
             two_max = jnp.max(jnp.where(low, -jnp.inf, part), axis=1, keepdims=True)
             parts.append(jnp.exp2(part - jnp.where(low, one_max, two_max)).astype(jnp.bfloat16))
-        p = jnp.concatenate(parts, axis=1)
-        both = dot(p, jnp.concatenate([vals, mask[...]], axis=1))
-        mix_s[g, rows, :] = both[:, :lane] / both[:, lane:]
+        return jnp.concatenate(parts, axis=1)
+
+    def mix(p, w, g):
+        v = qkv_s[2 * tiles + g, pl.ds(w, TOKENS, stride=GROUP), :].astype(jnp.bfloat16)
+        vals = jnp.concatenate([v] * several, axis=0) * mask[...]
+        return dot(p, jnp.concatenate([vals, mask[...]], axis=1))
 
     def step(n, _):
-        for w in range(4):
-            for g in range(tiles):
-                one(n * 4 + w, g)
+        items = [(n * 4 + w, g) for w in range(4) for g in range(tiles)]
+        found = [scores(w, g) for w, g in items]
+        found = [weights(s, g) for s, (_, g) in zip(found, items)]
+        found = [mix(p, w, g) for p, (w, g) in zip(found, items)]
+        for both, (w, g) in zip(found, items):
+            mix_s[g, pl.ds(w, TOKENS, stride=GROUP), :] = both[:, :lane] / both[:, lane:]
         return 0
 
     lax.fori_loop(0, GROUP // 4, step, 0)
 
 
-def feed_forward(i, block, x_s, mix_s, out_w, up_w, down_w):
-    rows = pl.ds(pl.multiple_of(i * block, block), block)
-    x = get(x_s, rows) + dot(get(mix_s, rows).astype(jnp.bfloat16), out_w[...])
-    x = x.astype(jnp.bfloat16).astype(jnp.float32)
-    inner = gelu(dot(norm(x), up_w[...]).astype(jnp.bfloat16))
-    return rows, x + dot(inner, down_w[...])
+def feed_forward(blocks, size, x_s, mix_s, out_w, up_w, down_w):
+    rows = [pl.ds(pl.multiple_of(i * size, size), size) for i in blocks]
+    xs = [get(x_s, r) + dot(get(mix_s, r).astype(jnp.bfloat16), out_w[...]) for r in rows]
+    xs = [x.astype(jnp.bfloat16).astype(jnp.float32) for x in xs]
+    normed = [norm(x) for x in xs]
+    part = 256
+    count = up_w.shape[1] // part
+    inner = [dot(v, up_w[:, :part]) for v in normed]
+    for b in range(count):
+        following = inner
+        if b + 1 < count:
+            following = [dot(v, up_w[:, (b + 1) * part : (b + 2) * part]) for v in normed]
+        lines = slice(b * part, (b + 1) * part)
+        xs = [
+            x + dot(gelu(v.astype(jnp.bfloat16)), down_w[lines, :]) for x, v in zip(xs, inner)
+        ]
+        inner = following
+    return list(zip(blocks, rows, xs))
 
 
 def neighbours():
@@ -135,32 +153,45 @@
     return result
 
 
-def convolve(k, starts, chunk_rows, pitch, stage, expand_w, dw, project_w, hidden, act, x_s):
+def convolve(k, starts, chunk_rows, pitch, stage, expand_w, dw, project_w, hidden, raw, x_s):
     channels = expand_w.shape[-1]
     span = SIDE + 2
 
-    def row(y, first, last):
+    def row(y):
         pieces = []
-        for t in range(first, last):
+        for t in range(span):
             for start in starts:
                 at = (start + k * chunk_rows + y) * pitch + SIDE - 1 + t
                 pieces.append(get(stage, pl.ds(at, SIDE, stride=SIDE)))
         return pieces
 
+    part = 256
+    count = channels // part
+
     def expand(n, _):
-        cells = jnp.concatenate(row(2 * n, 0, span) + row(2 * n + 1, 0, span), axis=0)
-        inner = gelu(dot(norm(cells), expand_w[...]).astype(jnp.bfloat16))
-        hidden[pl.ds(2 * n, 2)] = inner.reshape(2, span, GROUP, channels)
+        cells = jnp.concatenate(row(2 * n) + row(2 * n + 1), axis=0)
+        raw[pl.ds(2 * n, 2)] = cells.reshape(2, span, GROUP, cells.shape[1]).astype(jnp.bfloat16)
+        normed = norm(cells)
+        inner = dot(normed, expand_w[:, :part])
+        for b in range(count):
+            following = inner
+            if b + 1 < count:
+                following = dot(normed, expand_w[:, (b + 1) * part : (b + 2) * part])
+            hidden[pl.ds(2 * n, 2), :, :, b * part : (b + 1) * part] = gelu(
+                inner.astype(jnp.bfloat16)
+            ).reshape(2, span, GROUP, part)
+            inner = following
         return 0
 
     lax.fori_loop(0, span // 2, expand, 0)
-    size = SIDE * GROUP
+    size = 2 * SIDE * GROUP
 
     def depthwise(n, _):
-        for half in range(2):
-            y = 2 * n + half
-            for b in range(channels // 256):
-                lanes = slice(b * 256, (b + 1) * 256)
+        x = raw[pl.ds(2 * n + 1, 2), 1 : 1 + SIDE].astype(jnp.float32).reshape(size, raw.shape[3])
+        for b in range(count):
+            lanes = slice(b * part, (b + 1) * part)
+            both = []
+            for y in (2 * n, 2 * n + 1):
                 total = None
                 for dy in range(3):
                     for dx in range(3):
@@ -169,12 +200,9 @@
                             * dw[3 * dy + dx, :, lanes][None]
                         )
                         total = term if total is None else total + term
-                act[half * size : (half + 1) * size, lanes] = gelu(total).reshape(size, 256)
-        center = jnp.concatenate(
-            row(2 * n + 1, 1, 1 + SIDE) + row(2 * n + 2, 1, 1 + SIDE), axis=0
-        )
-        x = center + dot(act[...], project_w[...])
-        rows = pl.ds(pl.multiple_of(n * (2 * size), 2 * size), 2 * size)
+                both.append(gelu(total).reshape(size // 2, part))
+            x = x + dot(jnp.concatenate(both, axis=0), project_w[lanes, :])
+        rows = pl.ds(pl.multiple_of(n * size, size), size)
         put(x_s, rows, x.astype(jnp.bfloat16).astype(jnp.float32))
         return 0
 
@@ -187,7 +215,7 @@
     grid_qkv, grid_out, grid_bias, grid_up, grid_down,
     out,
     stage, edge, rows_in, cols_in, corners_in, mask, dw, edge_send, edge_recv,
-    hidden, act, x_s, qkv_s, mix_s, ready, arrived, result,
+    hidden, raw, x_s, qkv_s, mix_s, ready, arrived, result,
     send_go, recv_go, send_back, recv_back,
 ):
     chunks, devices, per, width = out.shape
@@ -280,30 +308,30 @@
 
     def block_chunk(k, _):
         convolve(
-            k, starts, chunk_rows, pitch, stage, expand_w, dw, project_w, hidden, act, x_s
+            k, starts, chunk_rows, pitch, stage, expand_w, dw, project_w, hidden, raw, x_s
         )
         attention(x_s, qkv_s, mix_s, blk_qkv, blk_bias, mask)
 
-        def step(n, _):
-            i = lax.rem(n + my_ha + 1, blocks)
-            rows, value = feed_forward(i, size, x_s, mix_s, blk_out, blk_up, blk_down)
+        def send(i, rows, value):
             put(x_s, rows, value)
             for w in range(GROUP):
                 strip, square = w // SIDE, w % SIDE
                 for h in range(SIDE // part_cols):
-                    first = h * part_cols * GROUP + w
-                    piece = jnp.concatenate(
-                        [
-                            get(
-                                x_s,
-                                pl.ds(
-                                    i * size + r * SIDE * GROUP + first, part_cols, stride=GROUP
-                                ),
-                            )
-                            for r in range(part_rows)
-                        ],
-                        axis=0,
-                    ).astype(jnp.bfloat16)
+                    first = i * size + h * part_cols * GROUP + w
+                    if part_cols == SIDE:
+                        piece = get(x_s, pl.ds(first, lines, stride=GROUP))
+                    else:
+                        piece = jnp.concatenate(
+                            [
+                                get(
+                                    x_s,
+                                    pl.ds(first + r * SIDE * GROUP, part_cols, stride=GROUP),
+                                )
+                                for r in range(part_rows)
+                            ],
+                            axis=0,
+                        )
+                    piece = piece.astype(jnp.bfloat16)
                     if lead == 2:
                         ready[k, i * n_wa + square, strip * lines : (strip + 1) * lines] = piece
                     else:
@@ -319,9 +347,15 @@
                 return 0
 
             lax.fori_loop(0, n_wa, go, 0)
+
+        def step(n, _):
+            pair = [lax.rem(2 * n + my_ha + 1 + o, blocks) for o in range(2)]
+            done = feed_forward(pair, size, x_s, mix_s, blk_out, blk_up, blk_down)
+            for i, rows, value in done:
+                send(i, rows, value)
             return 0
 
-        lax.fori_loop(0, blocks, step, 0)
+        lax.fori_loop(0, blocks // 2, step, 0)
         return 0
 
     lax.fori_loop(0, chunks, block_chunk, 0)
@@ -331,9 +365,7 @@
         put(x_s, slice(None), arrived[k].astype(jnp.float32).reshape(devices * per, width))
         attention(x_s, qkv_s, mix_s, grid_qkv, grid_bias, mask)
 
-        def step(n, _):
-            i = lax.rem(n + my_ha + 1, blocks)
-            rows, value = feed_forward(i, size, x_s, mix_s, grid_out, grid_up, grid_down)
+        def send(i, value):
             first = pl.multiple_of(i * share, share)
             result[k, pl.ds(first, share)] = value.reshape(share, per, width).astype(jnp.bfloat16)
 
@@ -343,9 +375,15 @@
                 return 0
 
             lax.fori_loop(0, share, go, 0)
+
+        def step(n, _):
+            pair = [lax.rem(2 * n + my_ha + 1 + o, blocks) for o in range(2)]
+            done = feed_forward(pair, size, x_s, mix_s, grid_out, grid_up, grid_down)
+            for i, _, value in done:
+                send(i, value)
             return 0
 
-        lax.fori_loop(0, blocks, step, 0)
+        lax.fori_loop(0, blocks // 2, step, 0)
         return 0
 
     lax.fori_loop(0, chunks, grid_chunk, 0)
@@ -358,7 +396,20 @@
     lax.fori_loop(0, chunks, finish, 0)
 
 
-def bias_kernel(tables, indices, *outs):
+def bias_kernel(lead, tables, blk_index, grid_index, *outs):
+    token = lax.broadcasted_iota(jnp.int32, (TOKENS, TOKENS), 0)
+    position = lax.broadcasted_iota(jnp.int32, (TOKENS, TOKENS), 1)
+    span = SIDE * lead
+    inside = lax.rem(token, span)
+    wanted = token - inside + SIDE * lax.rem(inside, lead) + lax.div(inside, lead)
+    order = (wanted == position).astype(jnp.float32)
+    ordered = lax.dot_general(
+        dot(order, grid_index[...].astype(jnp.float32)),
+        order,
+        (((1,), (1,)), ((), ())),
+        preferred_element_type=jnp.float32,
+    )
+    indices = [blk_index[...], (ordered + 0.5).astype(jnp.int32)]
     low = lax.broadcasted_iota(jnp.int32, (TOKENS, 2 * TOKENS), 1) < TOKENS
     for a in range(2):
         index = jnp.concatenate([indices[a], indices[a]], axis=1)
@@ -413,14 +464,12 @@
     strips = 2
     cells = GROUP * TOKENS
 
-    ordered = grid_index.reshape(n_ha, lead, SIDE, n_ha, lead, SIDE).transpose(0, 2, 1, 3, 5, 4)
-    indices = jnp.stack([blk_index, ordered.reshape(TOKENS, TOKENS)])
     tables = jnp.stack([blk_table, grid_table]).transpose(0, 2, 1)
     tables = jnp.pad(tables, ((0, 0), (0, 0), (0, 256 - tables.shape[2])))
     bias = pl.pallas_call(
-        bias_kernel,
+        functools.partial(bias_kernel, lead),
         out_shape=[jax.ShapeDtypeStruct((TOKENS, HEADS * TOKENS), jnp.float32)] * 2,
-    )(tables, indices)
+    )(tables, blk_index, grid_index)
     per = cells // (n_ha * n_wa)
     starts = [
         (m // (strips // lead)) * stride_rows + (m % (strips // lead)) * SIDE
@@ -446,7 +495,7 @@
             pltpu.SemaphoreType.DMA((8,)),
             pltpu.SemaphoreType.DMA((8,)),
             pltpu.VMEM((SIDE + 2, SIDE + 2, GROUP, channels), jnp.bfloat16),
-            pltpu.VMEM((2 * SIDE * GROUP, channels), jnp.bfloat16),
+            pltpu.VMEM((SIDE + 2, SIDE + 2, GROUP, width), jnp.bfloat16),
             pltpu.VMEM((width // 128, cells, 128), jnp.float32),
             pltpu.VMEM((3 * width // 128, cells, 128), jnp.float32),
             pltpu.VMEM((width // 128, cells, 128), jnp.float32),

time: 109 us -> 103 us (0.945)
  local copies, waits for them, and re-layouts: 6.7 us -> 3.36 us
  Pallas kernels: 101 us -> 99 us
    reshape x2 -> x0, local copies, waits for them, and re-layouts: 2.69 us -> none  [on_device(): grid_index.reshape(n_ha, lead, SIDE, n_ha, lead, SIDE)]
    pallas_call x1, Pallas kernels: 98.5 us -> 96.8 us  [on_device(): layer(field, expand_w, dw_kernel, project_w, blk_qkv, blk_out, bias[0], b...]
where the time goes in v2:
time: 103 us
  Pallas kernels  99 us (96%)
  local copies, waits for them, and re-layouts  3.36 us (3%)
    pallas_call x1, Pallas kernels, on_device(): layer(field, expand_w, dw_kernel, project_w, blk_qkv, blk_out, bias[0], b...  96.8 us
    transpose x1, local copies, waits for them, and re-layouts, on_device(): return updated.transpose(3, 0, 1, 4, 2, 5, 6).reshape(rows, cols, width)  2.76 us
    pallas_call x1, Pallas kernels, on_device(): pl.pallas_call(functools.partial(bias_kernel, lead), out_shape=[jax.Shape...  2.25 us

profile of v2, /device:TPU:0, one launch (start us, length us, event | category | flops | bytes accessed | tf_op | source)
XLA Modules:
  0.0 103.1 jit_solution(2365598498604648725)
XLA Ops:
  0.0 0.7 maximum_bitcast_fusion
  0.7 0.6 pad.4.tables
  1.3 2.2 %shard_map.154 = (f32[64,512]{1,0:T(8,128)}, f32[64,512]{1,0:T(8,128)}) custom-call(f32[2,8,256]{2,1,0:T(8,128)} %pad.4.tables, s32[64,64]{1,0:T(8,128)} %blk_index.1, s32[64,64]{1,0:T(8,128)} %grid_index.1), custom_call_target="tpu_custom_call" | custom-call | tf_op jit(solution)/shard_map/pallas_call | solution.py:469
  3.6 96.8 %shard_map.155 = bf16[3,32,32,256]{3,2,1,0:T(8,128)(2,1)} custom-call(bf16[48,64,256]{2,1,0:T(8,128)(2,1)} %field.1, bf16[256,1024]{1,0:T(8,128)(2,1)} %expand_w.1, f32[9,1024]{1,0:T(8,128)} %dw_kernel.1, bf16[1024,256]{1,0:T(8,128)(2,1)} %project_w.1, bf16[256,768]{1,0:T(8,128)(2,1)} %blk_qkv.1, bf16[256,256]{1,0:T(8,128)(2,1)} %blk_out.1, ...), custom_call_target="tpu_custom_call" | custom-call | flops 14495514624 | bytes 12582912 | tf_op jit(solution)/shard_map/pallas_call | solution.py:514
  100.3 2.8 %copy.17 = bf16[2,3,4,2,8,8,256]{6,5,4,3,2,1,0:T(8,128)(2,1)} copy(bf16[2,3,4,2,8,8,256]{6,5,3,0,4,2,1:T(8,128)(2,1)} %bitcast.8) | data formatting | bytes 3145728 | tf_op jit(solution)/shard_map/transpose | solution.py:519
